TPU v7x, 32 devices: a whole 2x2x4 slice. The times are simulated.
32 devices in a mesh: rows: 8 (over y, x, core), cols: 4 (over z).
Axes of the slice: x: 2, y: 2, z: 4, core: 2. Of those that a mesh axis runs over, the one named last changes fastest.
Arguments:
- basis: bfloat16 [32768, 512], P(('rows', 'cols')), may hold values from -6 to 6
- blocks: bfloat16 [256, 8, 128, 128], P(('rows', 'cols')), may hold values from -0.1875 to 0.1875
- neighbours: int32 [256, 8], P(('rows', 'cols')), may hold values from 0 to 255, as said below
- counts: int32 [256], P(('rows', 'cols')), may hold values from 3 to 8
- rotation: bfloat16 [512, 256], replicated, may hold values from -0.25 to 0.25
- ritz_values: float32 [256], replicated, may hold values from -2 to 2
Outputs:
- ritz: bfloat16 [32768, 256], P(('rows', 'cols'))
- ritz_image: bfloat16 [32768, 256], P(('rows', 'cols'))
- gram: float32 [512, 512], P('rows')
- projected: float32 [512, 512], P('rows')
- res_norm: float32 [256], replicated
Inputs may be any that keep to these rules, and one draw needn't show every extreme that they name: `neighbours`: every entry of row block b lies among the blocks of b's device and the one block just before and just after them: from 8 * (b // 8) - 1 to 8 * (b // 8) + 8; slot 0 is b itself; entries may repeat; entries at slots from counts[b] on are padding. `counts`: at least three slots are live.
All inputs are finite; a program needn't handle non-finite values.
Results may differ from a plain program's by a relative error of at most 0.015.
Values may be sent and summed in bfloat16 or wider, within the bound.
A program may use at most 64 MiB of HBM per device.

v0:
```python
import jax
import jax.numpy as jnp
from jax import lax
from jax.sharding import PartitionSpec as P


def extended(block, sides, width):
    for axis, dim in sides:
        count = lax.axis_size(axis)
        forward = [(i, i + 1) for i in range(count - 1)]
        backward = [(target, source) for source, target in forward]
        low = lax.ppermute(
            lax.slice_in_dim(block, block.shape[dim] - width, None, axis=dim), axis, forward
        )
        high = lax.ppermute(lax.slice_in_dim(block, 0, width, axis=dim), axis, backward)
        block = jnp.concatenate([low, block, high], axis=dim)
    return block


def body(basis, blocks, neighbours, counts, rotation, ritz_values):
    count_blocks = blocks.shape[0]
    slots = blocks.shape[1]
    size_block = blocks.shape[2]
    width = basis.shape[1]
    devices = lax.axis_size("rows") * lax.axis_size("cols")
    rows_total = basis.shape[0] * devices
    first = lax.axis_index(("rows", "cols")) * count_blocks - 1
    local_index = neighbours - first
    live = jnp.arange(slots, dtype=jnp.int32)[None, :] < counts[:, None]
    masked = jnp.where(live[:, :, None, None], blocks, jnp.zeros_like(blocks))
    total = jnp.zeros((count_blocks, size_block, width), jnp.float32)
    own = basis.reshape(count_blocks, size_block, width)
    inside = (local_index >= 1) & (local_index <= count_blocks)
    for slot in range(slots):
        picked = own[jnp.clip(local_index[:, slot] - 1, 0, count_blocks - 1)]
        held = jnp.where(
            inside[:, slot][:, None, None], masked[:, slot], jnp.zeros_like(masked[:, slot])
        )
        total = total + jnp.einsum("brs,bsk->brk", held, picked, preferred_element_type=jnp.float32)
    padded = extended(basis, ((("rows", "cols"), 0),), size_block)
    lower_rows = padded[:size_block]
    upper_rows = padded[-size_block:]
    zero_block = jnp.zeros_like(masked)
    below = jnp.sum(jnp.where((local_index == 0)[:, :, None, None], masked, zero_block), axis=1)
    above = jnp.sum(
        jnp.where((local_index == count_blocks + 1)[:, :, None, None], masked, zero_block), axis=1
    )
    total = total + jnp.einsum("brs,sk->brk", below, lower_rows, preferred_element_type=jnp.float32)
    total = total + jnp.einsum("brs,sk->brk", above, upper_rows, preferred_element_type=jnp.float32)
    image = total.reshape(basis.shape[0], width).astype(jnp.bfloat16)
    joined = jnp.concatenate([basis, image], axis=1)
    partial_rows = lax.psum_scatter(
        jnp.dot(basis.T, joined, preferred_element_type=jnp.float32) / rows_total,
        "rows",
        scatter_dimension=0,
        tiled=True,
    )
    both = lax.psum(partial_rows.astype(jnp.bfloat16), "cols").astype(jnp.float32)
    gram = both[:, :width]
    projected = both[:, width:]
    ritz_full = jnp.dot(basis, rotation, preferred_element_type=jnp.float32)
    image_full = jnp.dot(image, rotation, preferred_element_type=jnp.float32)
    resid = image_full - ritz_values[None, :] * ritz_full
    squares = lax.psum(jnp.sum(resid * resid, axis=0), ("rows", "cols"))
    res_norm = jnp.sqrt(squares / rows_total)
    return (
        ritz_full.astype(jnp.bfloat16),
        image_full.astype(jnp.bfloat16),
        gram,
        projected,
        res_norm,
    )


def solution(mesh):
    return jax.shard_map(
        body,
        mesh=mesh,
        in_specs=(
            P(("rows", "cols"), None),
            P(("rows", "cols"), None, None, None),
            P(("rows", "cols"), None),
            P(("rows", "cols")),
            P(),
            P(),
        ),
        out_specs=(
            P(("rows", "cols"), None),
            P(("rows", "cols"), None),
            P("rows", None),
            P("rows", None),
            P(),
        ),
        check_vma=False,
    )
```

profile of v0, /device:TPU:0, one launch (start us, length us, event | category | flops | bytes accessed | tf_op | source)
XLA Modules:
  0.0 140.9 jit_solution(16408295484630463374)
XLA Ops:
  7.2 1.8 %fusion.69 = (bf16[128,512]{1,0:T(8,128)(2,1)}, bf16[128,512]{1,0:T(8,128)(2,1)}) fusion(bf16[1024,512]{1,0:T(8,128)(2,1)} %param.6), kind=kLoop, calls=%fused_computation.109 | loop fusion | bytes 524288 | tf_op jit(solution)/shard_map/slice | solution.py:15
  9.0 5.6 %collective-permute-start = (bf16[128,512]{1,0:T(8,128)(2,1)}, bf16[128,512]{1,0:T(8,128)(2,1)}, u32[]{:S(2)}, u32[]{:S(2)}) collective-permute-start(bf16[128,512]{1,0:T(8,128)(2,1)} %get-tuple-element.40), channel_id=1, source_target_pairs={{0,1},{1,2},{2,3},{3,4},{4,5},{5,6},{6,7},{7,8},{8,9},{9,10},{10,1... | collective-permute-start | bytes 393224 | tf_op jit(solution)/shard_map/ppermute | solution.py:12
  14.6 1.3 collective-permute-start.1
  16.6 0.8 fusion.53
  17.4 1.3 broadcast_compare_fusion.1
  18.7 0.8 slice_reduce_fusion.6
  19.5 1.8 %gather_fusion.6 = bf16[8,128,512]{2,1,0:T(8,128)(2,1)S(1)} fusion(bf16[8,128,512]{2,1,0:T(8,128)(2,1)} %bitcast.82, s32[1024]{0:T(1024)S(1)} %get-tuple-element.48), kind=kCustom, calls=%fused_computation.6 | custom fusion | bytes 2097184 | tf_op jit(solution)/shard_map/gather | solution.py:35
  22.0 1.6 %gather_fusion.4 = bf16[8,128,512]{2,1,0:T(8,128)(2,1)} fusion(bf16[8,128,512]{2,1,0:T(8,128)(2,1)S(1)} %bitcast.84, s32[1024]{0:T(1024)S(1)} %get-tuple-element.50), kind=kCustom, calls=%fused_computation.4 | custom fusion | bytes 2097184 | tf_op jit(solution)/shard_map/gather | solution.py:35
  24.2 1.6 %gather_fusion.3 = bf16[8,128,512]{2,1,0:T(8,128)(2,1)} fusion(bf16[8,128,512]{2,1,0:T(8,128)(2,1)S(1)} %bitcast.85, s32[1024]{0:T(1024)S(1)} %get-tuple-element.51), kind=kCustom, calls=%fused_computation.3 | custom fusion | bytes 2097184 | tf_op jit(solution)/shard_map/gather | solution.py:35
  25.9 1.6 %gather_fusion.2 = bf16[8,128,512]{2,1,0:T(8,128)(2,1)} fusion(bf16[8,128,512]{2,1,0:T(8,128)(2,1)S(1)} %bitcast.86, s32[1024]{0:T(1024)S(1)} %get-tuple-element.52), kind=kCustom, calls=%fused_computation.2 | custom fusion | bytes 2097184 | tf_op jit(solution)/shard_map/gather | solution.py:35
  28.1 1.6 %gather_fusion.1 = bf16[8,128,512]{2,1,0:T(8,128)(2,1)} fusion(bf16[8,128,512]{2,1,0:T(8,128)(2,1)S(1)} %bitcast.87, s32[1024]{0:T(1024)S(1)} %get-tuple-element.53), kind=kCustom, calls=%fused_computation.1 | custom fusion | bytes 2097184 | tf_op jit(solution)/shard_map/gather | solution.py:35
  29.7 1.6 %gather_fusion = bf16[8,128,512]{2,1,0:T(8,128)(2,1)} fusion(bf16[8,128,512]{2,1,0:T(8,128)(2,1)S(1)} %bitcast.88, s32[1024]{0:T(1024)S(1)} %get-tuple-element.54), kind=kCustom, calls=%fused_computation | custom fusion | bytes 2097184 | tf_op jit(solution)/shard_map/gather | solution.py:35
  31.4 1.6 %gather_fusion.7 = bf16[8,128,512]{2,1,0:T(8,128)(2,1)} fusion(bf16[8,128,512]{2,1,0:T(8,128)(2,1)S(1)} %bitcast.89, s32[1024]{0:T(1024)S(1)} %get-tuple-element.47), kind=kCustom, calls=%fused_computation.7 | custom fusion | bytes 2097184 | tf_op jit(solution)/shard_map/gather | solution.py:35
  33.0 2.8 %select_reduce_fusion = (bf16[8,128,128]{2,1,0:T(8,128)(2,1)S(1)}, bf16[8,128,128]{2,1,0:T(8,128)(2,1)S(1)}, bf16[8,8,128,128]{3,2,1,0:T(8,128)(2,1)S(1)}) fusion(pred[8,8]{1,0:T(8,128)(4,1)S(1)} %copy-done.8, pred[8,8]{1,0:T(8,128)(4,1)S(1)} %get-tuple-element.43, bf16[8,8,128,128]{3,2,1,0:T(8,128)(2,1)} %param.7, pred[8,8]{1,0:T(8,128)(4,1)S(1)} %copy-done.9), kind=kLoop, calls=%fused_computation.14 | loop fusion | flops 4980736 | bytes 4718784 | tf_op jit(solution)/shard_map/reduce_sum | solution.py:45
  42.2 1.3 fusion.42
  43.5 0.9 add_convert_fusion
  44.5 2.6 %multiply_bitcast_fusion = f32[512,1024]{0,1:T(8,128)} fusion(bf16[1024,512]{1,0:T(8,128)(2,1)S(1)} %copy-done.1, bf16[1024,512]{1,0:T(8,128)(2,1)S(1)} %bitcast.90), kind=kOutput, calls=%fused_computation.12 | convolution fusion | flops 1078460416 | bytes 4194304 | tf_op jit(solution)/shard_map/dot_general | solution.py:53
  47.1 2.9 %copy.29 = f32[512,1024]{1,0:T(8,128)} copy(f32[512,1024]{0,1:T(8,128)} %multiply_bitcast_fusion) | data formatting | bytes 4194304
  50.7 1.4 multiply_reduce_fusion
  52.1 41.0 %psum.15 = f32[256]{0:T(256)S(1)} all-reduce(f32[256]{0:T(256)S(1)} %get-tuple-element.36), channel_id=1, replica_groups=mesh['rows'=8,'cols'=4] {'rows','cols'}, use_global_device_ids=true, to_apply=%region_5.6 | all-reduce | flops 256 | bytes 2048 | tf_op jit(solution)/shard_map/psum | solution.py:64
  93.7 1.8 %copy.30 = bf16[64,1024]{0,1:T(8,128)(2,1)} copy(f32[64,1024]{1,0:T(8,128)} %reduce-scatter.4.cloned.1.call-done) | data formatting | bytes 393216
  96.1 35.4 %all-reduce.2.cloned.1.call-done = bf16[64,1024]{0,1:T(8,128)(2,1)} async-done(((bf16[64,1024]{0,1:T(8,128)(2,1)}), bf16[64,1024]{0,1:T(8,128)(2,1)}) %all-reduce.2.cloned.1.call-update) | async-done | bytes 131088 | tf_op jit(solution)/shard_map/psum | solution.py:58
  131.5 1.0 fusion.70
  132.5 0.8 copy.27
  (62 shorter events, 11.6 us)
Async XLA Ops:
  7.2 42.9 %copy-start = (bf16[512,256]{1,0:T(8,128)(2,1)S(1)}, bf16[512,256]{1,0:T(8,128)(2,1)}, u32[]{:S(2)}) copy-start(bf16[512,256]{1,0:T(8,128)(2,1)} %param.10) | copy-start | bytes 786436
  7.2 14.2 %copy-start.1 = (bf16[1024,512]{1,0:T(8,128)(2,1)S(1)}, bf16[1024,512]{1,0:T(8,128)(2,1)}, u32[]{:S(2)}) copy-start(bf16[1024,512]{1,0:T(8,128)(2,1)} %param.6) | copy-start | bytes 3145732
  7.2 86.5 %reduce-scatter.4.cloned.1.call-start = ((), (), s32[]{:S(2)}) async-start(), calls=%async_computation.2 | async-start | bytes 2359296
  9.0 33.2 %collective-permute-start = (bf16[128,512]{1,0:T(8,128)(2,1)}, bf16[128,512]{1,0:T(8,128)(2,1)}, u32[]{:S(2)}, u32[]{:S(2)}) collective-permute-start(bf16[128,512]{1,0:T(8,128)(2,1)} %get-tuple-element.40), channel_id=1, source_target_pairs={{0,1},{1,2},{2,3},{3,4},{4,5},{5,6},{6,7},{7,8},{8,9},{9,10},{10,1... | collective-permute-start | bytes 393224 | tf_op jit(solution)/shard_map/ppermute | solution.py:12
  14.6 29.0 %collective-permute-start.1 = (bf16[128,512]{1,0:T(8,128)(2,1)}, bf16[128,512]{1,0:T(8,128)(2,1)S(1)}, u32[]{:S(2)}, u32[]{:S(2)}) collective-permute-start(bf16[128,512]{1,0:T(8,128)(2,1)} %get-tuple-element.39), channel_id=1, source_target_pairs={{1,0},{2,1},{3,2},{4,3},{5,4},{6,5},{7,6},{8,7},{9,8},{10,9},{11,1... | collective-permute-start | bytes 393224 | tf_op jit(solution)/shard_map/ppermute | solution.py:15
  29.7 3.3 %copy-start.8 = (pred[8,8]{1,0:T(8,128)(4,1)S(1)}, pred[8,8]{1,0:T(8,128)(4,1)}, u32[]{:S(2)}) copy-start(pred[8,8]{1,0:T(8,128)(4,1)} %get-tuple-element.44) | copy-start | bytes 196
  31.4 1.6 %copy-start.9 = (pred[8,8]{1,0:T(8,128)(4,1)S(1)}, pred[8,8]{1,0:T(8,128)(4,1)}, u32[]{:S(2)}) copy-start(pred[8,8]{1,0:T(8,128)(4,1)} %get-tuple-element.46) | copy-start | bytes 196
  33.0 2.8 %copy-start.17 = (pred[8]{0:T(512)(128)(4,1)S(1)}, pred[8]{0:T(512)(128)(4,1)}, u32[]{:S(2)}) copy-start(pred[8]{0:T(512)(128)(4,1)} %get-tuple-element.27) | copy-start | bytes 28
  35.8 0.6 copy-start.16
  36.3 1.2 copy-start.2
  36.3 1.2 copy-start.15
  36.9 1.3 copy-start.3
  36.9 1.3 copy-start.14
  38.0 1.3 copy-start.4
  38.0 1.3 copy-start.13
  38.6 1.3 copy-start.6
  38.6 1.3 copy-start.12
  39.7 1.3 copy-start.7
  39.7 1.3 copy-start.11
  40.4 1.3 copy-start.5
  40.4 1.3 copy-start.10
  50.0 0.7 copy-start.18
  50.0 81.4 %all-reduce.2.cloned.1.call-start = ((), (), s32[]{:S(2)}) async-start(), calls=%async_computation.1 | async-start | bytes 524288 | tf_op jit(solution)/shard_map/psum | solution.py:58
Sparse Core Ops, SparseCore 0:
  50.2 43.5 reduce-scatter.3
  96.2 35.2 all-reduce.1
where the time goes:
time: 141 us
  blocking collectives  41 us (29%)
  waiting for transfers between devices  36.1 us (26%)
  local copies, waits for them, and re-layouts  24.7 us (18%)
  between operations  14.3 us (10%)
  matrix products  10.5 us (7%)
  other arithmetic  7.46 us (5%)
  starting transfers between devices  6.93 us (5%)
    psum x1, blocking collectives, body(): squares = lax.psum(jnp.sum(resid * resid, axis=0), ('rows', 'cols'))  41 us
    psum x1, waiting for transfers between devices, body(): lax.psum(partial_rows.astype(jnp.bfloat16), 'cols').astype(jnp.float32)  35.4 us
    gather x8, local copies, waits for them, and re-layouts, body(): picked = own[jnp.clip(local_index[:, slot] - 1, 0, count_blocks - 1)]  12.1 us
    unnamed x42, local copies, waits for them, and re-layouts  8.96 us
    ppermute x1, starting transfers between devices, extended(): lax.ppermute(lax.slice_in_dim(block, block.shape[dim] - width, None, axis...  5.57 us
    dot_general x8, matrix products, body(): jnp.einsum('brs,bsk->brk', held, picked, preferred_element_type=jnp.float32)  3.79 us
  transfers between devices with their start and end apart: 4, of which 2 were waited for; matrix products, arithmetic and copies ran while one was open for 19% of the time, Pallas kernels for 0%

commit v1 on v0

--- a/solution.py
+++ b/solution.py
@@ -1,6 +1,10 @@
+import functools
+
 import jax
 import jax.numpy as jnp
 from jax import lax
+from jax.experimental import pallas as pl
+from jax.experimental.pallas import tpu as pltpu
 from jax.sharding import PartitionSpec as P
 
 
@@ -17,7 +21,7 @@
     return block
 
 
-def body(basis, blocks, neighbours, counts, rotation, ritz_values):
+def general_body(basis, blocks, neighbours, counts, rotation, ritz_values):
     count_blocks = blocks.shape[0]
     slots = blocks.shape[1]
     size_block = blocks.shape[2]
@@ -72,6 +76,299 @@
     )
 
 
+BF16, F32 = jnp.bfloat16, jnp.float32
+
+
+def dot(a, b):
+    return jnp.dot(a, b, preferred_element_type=F32)
+
+
+def fold(x):
+    return jnp.sum(x.reshape(x.shape[0] // 8, 8, x.shape[1]), axis=0)
+
+
+def kernel(
+    sizes, nbr, cnt, basis_hbm, blocks_hbm, rot, vals,
+    ritz_hbm, rimg_hbm, gram_out, proj_out, res_out,
+    own, blk, mat_in, mat_halo, halo, acc, image, bt, rfull, ritz_v, rimg_v,
+    half, core_send, core_recv, part, plane_send, plane_recv,
+    z_send, z_recv, gat, sq_own, sq_core, sq_plane, sq_z,
+    local_sem, halo_ss, halo_rs, core_ss, core_rs, plane_ss, plane_rs,
+    zs_ss, zs_rs, za_ss, za_rs,
+):
+    nb, nnb, bs, k, m, R, Z = sizes
+    Q = R // 2
+    rows = nb * bs
+    chunk = k // R
+    piece = chunk // Z
+    rows_total = rows * R * Z
+    r = lax.axis_index("rows")
+    z = lax.axis_index("cols")
+    c = lax.rem(r, 2)
+    q = r // 2
+    me = r * Z + z
+    first = me * nb - 1
+
+    def at(index):
+        return (index // Z, lax.rem(index, Z))
+
+    ahead = at(lax.rem(me + 1, R * Z))
+    behind = at(lax.rem(me + R * Z - 1, R * Z))
+    mate = (q * 2 + 1 - c, z)
+    plane_q = [lax.rem(q + d, Q) for d in range(1, Q)]
+    plane = [(p * 2 + c, z) for p in plane_q]
+    line_z = [lax.rem(z + d, Z) for d in range(1, Z)]
+    line = [(r, p) for p in line_z]
+
+    get_basis = pltpu.make_async_copy(basis_hbm, own, local_sem.at[0])
+    get_basis.start()
+    get_blocks = pltpu.make_async_copy(blocks_hbm, blk, local_sem.at[1])
+    get_blocks.start()
+
+    barrier = pltpu.get_barrier_semaphore()
+    peers = [ahead, behind, mate] + plane + line
+    for peer in peers:
+        pl.semaphore_signal(barrier, inc=1, device_id=peer, device_id_type=pl.DeviceIdType.MESH)
+    pl.semaphore_wait(barrier, len(peers))
+
+    sends = []
+
+    def remote(src, dst, ss, rs, to):
+        copy = pltpu.make_async_remote_copy(
+            src_ref=src, dst_ref=dst, send_sem=ss, recv_sem=rs,
+            device_id=to, device_id_type=pl.DeviceIdType.MESH,
+        )
+        copy.start()
+        sends.append(copy)
+        return copy
+
+    halo_copies = [
+        remote(basis_hbm.at[pl.ds(rows - bs, bs)], halo.at[pl.ds(0, bs)],
+               halo_ss.at[0], halo_rs.at[0], ahead),
+        remote(basis_hbm.at[pl.ds(0, bs)], halo.at[pl.ds(bs, bs)],
+               halo_ss.at[1], halo_rs.at[1], behind),
+    ]
+
+    get_basis.wait()
+    for i in range(Q):
+        turned = own[:, i * 2 * chunk:(i + 1) * 2 * chunk].T
+        for side in range(2):
+            bt[side, pl.ds(i * chunk, chunk), :] = turned[side * chunk:(side + 1) * chunk]
+
+    def core_phase(which, right):
+        core_send[which] = dot(bt[1 - c], right[...]).astype(BF16)
+        copy = remote(core_send.at[which], core_recv.at[which], core_ss.at[which],
+                      core_rs.at[which], mate)
+        half[which] = dot(bt[c], right[...])
+        return copy
+
+    def plane_phase(which, core_copy):
+        core_copy.wait_recv()
+        total = half[which] + core_recv[which].astype(F32)
+        half[which] = total
+        plane_send[which] = total.astype(BF16).reshape(Q, chunk, k)
+        return [
+            remote(plane_send.at[which, plane_q[d]], plane_recv.at[which, d],
+                   plane_ss.at[which, d], plane_rs.at[which, d], plane[d])
+            for d in range(Q - 1)
+        ]
+
+    def line_phase(which, copies):
+        total = half[which, pl.ds(pl.multiple_of(q * chunk, chunk), chunk), :]
+        for d, copy in enumerate(copies):
+            copy.wait_recv()
+            total = total + plane_recv[which, d].astype(F32)
+        part[which] = total
+        z_send[which] = total.astype(BF16).reshape(Z, piece, k)
+        return [
+            remote(z_send.at[which, line_z[d]], z_recv.at[which, d],
+                   zs_ss.at[which, d], zs_rs.at[which, d], line[d])
+            for d in range(Z - 1)
+        ]
+
+    def gather_phase(which, copies):
+        total = part[which, pl.ds(pl.multiple_of(z * piece, piece), piece), :]
+        for d, copy in enumerate(copies):
+            copy.wait_recv()
+            total = total + z_recv[which, d].astype(F32)
+        gat[which, z] = total.astype(BF16)
+        return [
+            remote(gat.at[which, z], gat.at[which, z],
+                   za_ss.at[which, d], za_rs.at[which, d], line[d])
+            for d in range(Z - 1)
+        ]
+
+    def finish(which, copies, out):
+        for copy in copies:
+            copy.wait_recv()
+        out[...] = gat[which].astype(F32).reshape(chunk, k) / rows_total
+
+    gram_core = core_phase(0, own)
+
+    rfull[...] = dot(own[...], rot[...])
+    ritz_v[...] = rfull[...].astype(BF16)
+    put_ritz = pltpu.make_async_copy(ritz_v, ritz_hbm, local_sem.at[2])
+    put_ritz.start()
+
+    get_blocks.wait()
+
+    @pl.loop(0, nb)
+    def _(b):
+        n = cnt[b]
+        spot = [jnp.where(j < n, nbr[b, j] - first, -1) for j in range(nnb)]
+        tiles = [blk[b, j] for j in range(nnb)]
+        there = pl.ds(pl.multiple_of(b * bs, bs), bs)
+        for s in range(nb + 2):
+            total = jnp.zeros((bs, bs), BF16)
+            for j in range(nnb):
+                weight = jnp.where(spot[j] == s, 1.0, 0.0).astype(F32)
+                total = total + tiles[j] * jnp.full((bs, bs), weight, F32).astype(BF16)
+            if s == 0:
+                mat_halo[there, 0:bs] = total
+            elif s == nb + 1:
+                mat_halo[there, bs:2 * bs] = total
+            else:
+                mat_in[there, (s - 1) * bs:s * bs] = total
+
+    gram_plane = plane_phase(0, gram_core)
+
+    step = min(rows, 2 * bs)
+
+    @pl.loop(0, rows // step)
+    def _(i):
+        there = pl.ds(pl.multiple_of(i * step, step), step)
+        acc[there, :] = dot(mat_in[there, :], own[...])
+
+    gram_line = line_phase(0, gram_plane)
+
+    for copy in halo_copies:
+        copy.wait_recv()
+
+    @pl.loop(0, rows // step)
+    def _(i):
+        there = pl.ds(pl.multiple_of(i * step, step), step)
+        image[there, :] = (acc[there, :] + dot(mat_halo[there, :], halo[...])).astype(BF16)
+
+    proj_core = core_phase(1, image)
+    gram_gather = gather_phase(0, gram_line)
+
+    sq_own[...] = jnp.zeros_like(sq_own)
+
+    @pl.loop(0, rows // step)
+    def _(i):
+        there = pl.ds(pl.multiple_of(i * step, step), step)
+        full = dot(image[there, :], rot[...])
+        rimg_v[there, :] = full.astype(BF16)
+        resid = full - vals[...] * rfull[there, :]
+        sq_own[...] += fold(resid * resid)
+
+    put_rimg = pltpu.make_async_copy(rimg_v, rimg_hbm, local_sem.at[3])
+    put_rimg.start()
+    sq_copy = remote(sq_own, sq_core, core_ss.at[2], core_rs.at[2], mate)
+
+    proj_plane = plane_phase(1, proj_core)
+    sq_copy.wait_recv()
+    sq_plane[q] = sq_own[...] + sq_core[...]
+    sq_copies = [
+        remote(sq_plane.at[q], sq_plane.at[q], plane_ss.at[2, d], plane_rs.at[2, d], plane[d])
+        for d in range(Q - 1)
+    ]
+    finish(0, gram_gather, gram_out)
+    proj_line = line_phase(1, proj_plane)
+    for copy in sq_copies:
+        copy.wait_recv()
+    sq_z[z] = jnp.sum(sq_plane[...], axis=0)
+    sq_copies = [
+        remote(sq_z.at[z], sq_z.at[z], za_ss.at[2, d], za_rs.at[2, d], line[d])
+        for d in range(Z - 1)
+    ]
+    proj_gather = gather_phase(1, proj_line)
+    for copy in sq_copies:
+        copy.wait_recv()
+    squares = jnp.sum(jnp.sum(sq_z[...], axis=0), axis=0, keepdims=True)
+    res_out[...] = jnp.sqrt(squares / rows_total)
+    finish(1, proj_gather, proj_out)
+    for copy in sends:
+        copy.wait_send()
+    put_ritz.wait()
+    put_rimg.wait()
+
+
+def fused_body(basis, blocks, neighbours, counts, rotation, ritz_values):
+    R, Z = lax.axis_size("rows"), lax.axis_size("cols")
+    nb, nnb, bs, _ = blocks.shape
+    rows, k = basis.shape
+    m = rotation.shape[1]
+    Q, chunk, piece = R // 2, k // R, k // R // Z
+    vmem = pltpu.VMEM
+    dma = pltpu.SemaphoreType.DMA
+    any_spec = pl.BlockSpec(memory_space=pl.ANY)
+    smem_spec = pl.BlockSpec(memory_space=pltpu.SMEM)
+    vmem_spec = pl.BlockSpec(memory_space=pltpu.VMEM)
+    ritz, rimg, gram, proj, res = pl.pallas_call(
+        functools.partial(kernel, (nb, nnb, bs, k, m, R, Z)),
+        out_shape=(
+            jax.ShapeDtypeStruct((rows, m), BF16),
+            jax.ShapeDtypeStruct((rows, m), BF16),
+            jax.ShapeDtypeStruct((chunk, k), F32),
+            jax.ShapeDtypeStruct((chunk, k), F32),
+            jax.ShapeDtypeStruct((1, m), F32),
+        ),
+        in_specs=[smem_spec, smem_spec, any_spec, any_spec, vmem_spec, vmem_spec],
+        out_specs=(any_spec, any_spec, vmem_spec, vmem_spec, vmem_spec),
+        scratch_shapes=[
+            vmem((rows, k), BF16),
+            vmem((nb, nnb, bs, bs), BF16),
+            vmem((rows, nb * bs), BF16),
+            vmem((rows, 2 * bs), BF16),
+            vmem((2 * bs, k), BF16),
+            vmem((rows, k), F32),
+            vmem((rows, k), BF16),
+            vmem((2, k // 2, rows), BF16),
+            vmem((rows, m), F32),
+            vmem((rows, m), BF16),
+            vmem((rows, m), BF16),
+            vmem((2, k // 2, k), F32),
+            vmem((2, k // 2, k), BF16),
+            vmem((2, k // 2, k), BF16),
+            vmem((2, chunk, k), F32),
+            vmem((2, Q, chunk, k), BF16),
+            vmem((2, Q - 1, chunk, k), BF16),
+            vmem((2, Z, piece, k), BF16),
+            vmem((2, Z - 1, piece, k), BF16),
+            vmem((2, Z, piece, k), BF16),
+            vmem((8, m), F32),
+            vmem((8, m), F32),
+            vmem((Q, 8, m), F32),
+            vmem((Z, 8, m), F32),
+            dma((4,)),
+            dma((2,)),
+            dma((2,)),
+            dma((3,)),
+            dma((3,)),
+            dma((3, Q - 1)),
+            dma((3, Q - 1)),
+            dma((2, Z - 1)),
+            dma((2, Z - 1)),
+            dma((3, Z - 1)),
+            dma((3, Z - 1)),
+        ],
+        compiler_params=pltpu.CompilerParams(
+            collective_id=0, has_side_effects=True, vmem_limit_bytes=40 * 1024 * 1024
+        ),
+        name="davidson_step",
+    )(neighbours, counts, basis, blocks, rotation, ritz_values.reshape(1, m))
+    return ritz, rimg, gram, proj, res.reshape(m)
+
+
+def body(basis, blocks, neighbours, counts, rotation, ritz_values):
+    R, Z = lax.axis_size("rows"), lax.axis_size("cols")
+    k = basis.shape[1]
+    even = R % 4 == 0 and Z > 1 and k % (16 * R * Z) == 0 and (2 * k // R) % 128 == 0
+    chosen = fused_body if even else general_body
+    return chosen(basis, blocks, neighbours, counts, rotation, ritz_values)
+
+
 def solution(mesh):
     return jax.shard_map(
         body,

time: 141 us -> 44.4 us (0.31)
  blocking collectives: 41 us -> 0 us
  waiting for transfers between devices: 36.1 us -> 0 us
  Pallas kernels: 0 us -> 34.3 us
  local copies, waits for them, and re-layouts: 24.7 us -> 9.24 us
  between operations: 14.3 us -> 0.66 us
  matrix products: 10.5 us -> 0 us
  other arithmetic: 7.46 us -> 0 us
  starting transfers between devices: 6.93 us -> 0 us
    psum x1 -> x0, blocking collectives: 41 us -> none  [body(): squares = lax.psum(jnp.sum(resid * resid, axis=0), ('rows', 'cols'))]
    psum x1 -> x0, waiting for transfers between devices: 35.4 us -> none  [body(): lax.psum(partial_rows.astype(jnp.bfloat16), 'cols').astype(jnp.float32)]
    pallas_call x0 -> x1, Pallas kernels: none -> 34.3 us  [fused_body(): pl.pallas_call(functools.partial(kernel, (nb, nnb, bs, k, m, R, Z)), out_...]
    gather x8 -> x0, local copies, waits for them, and re-layouts: 12.1 us -> none  [body(): picked = own[jnp.clip(local_index[:, slot] - 1, 0, count_blocks - 1)]]
    dot_general x13 -> x0, matrix products: 10.5 us -> none  [the longest x8 3.79 us: body(): jnp.einsum('brs,bsk->brk', held, picked, preferred_element_type=jnp.float32)]
    ppermute x2 -> x0, starting transfers between devices: 6.85 us -> none  [the longest x1 5.57 us: extended(): lax.ppermute(lax.slice_in_dim(block, block.shape[dim] - width, None, axis...]
    slice x3 -> x0, local copies, waits for them, and re-layouts: 3.62 us -> none  [the longest x1 1.78 us: extended(): lax.slice_in_dim(block, 0, width, axis=dim)]
    reduce_sum x1 -> x0, other arithmetic: 2.79 us -> none  [body(): jnp.sum(jnp.where((local_index == count_blocks + 1)[:, :, None, None], ma...]
  transfers between devices with their start and end apart: 4 -> 0, of which waited for: 2 -> 0; matrix products, arithmetic and copies ran while one was open for 19% -> 0% of each run, Pallas kernels for 0% -> 0%
where the time goes in v1:
time: 44.4 us; the launch traced here: 44.2 us
  Pallas kernels  34.3 us (77%)
  local copies, waits for them, and re-layouts  9.24 us (21%)
  between operations  0.66 us (1%)
    pallas_call x1, Pallas kernels, fused_body(): pl.pallas_call(functools.partial(kernel, (nb, nnb, bs, k, m, R, Z)), out_...  34.3 us
    unnamed x17, local copies, waits for them, and re-layouts  9.24 us

profile of v1, /device:TPU:0, one launch (start us, length us, event | category | flops | bytes accessed | tf_op | source)
XLA Modules:
  0.0 44.2 jit_solution(801445371104790230)
XLA Ops:
  0.6 0.0 copy-start
  0.6 1.6 %copy-done = bf16[8,8,128,128]{3,2,1,0:T(8,128)(2,1)S(1)} copy-done((bf16[8,8,128,128]{3,2,1,0:T(8,128)(2,1)S(1)}, bf16[8,8,128,128]{3,2,1,0:T(8,128)(2,1)}, u32[]{:S(2)}) %copy-start) | copy-done | bytes 2097176
  2.2 0.0 copy-start.1
  2.2 1.2 %copy-done.1 = bf16[1024,512]{1,0:T(8,128)(2,1)S(1)} copy-done((bf16[1024,512]{1,0:T(8,128)(2,1)S(1)}, bf16[1024,512]{1,0:T(8,128)(2,1)}, u32[]{:S(2)}) %copy-start.1) | copy-done | bytes 1048600
  3.5 0.0 copy-start.2
  3.5 0.9 %copy-done.2 = bf16[512,256]{1,0:T(8,128)(2,1)S(1)} copy-done((bf16[512,256]{1,0:T(8,128)(2,1)S(1)}, bf16[512,256]{1,0:T(8,128)(2,1)}, u32[]{:S(2)}) %copy-start.2) | copy-done | bytes 262168
  4.4 0.0 copy-start.3
  4.4 0.7 %copy-done.3 = s32[8,8]{1,0:T(8,128)S(1)} copy-done((s32[8,8]{1,0:T(8,128)S(1)}, s32[8,8]{1,0:T(8,128)}, u32[]{:S(2)}) %copy-start.3) | copy-done | bytes 280
  5.1 0.0 copy-start.4
  5.1 0.7 %copy-done.4 = f32[256]{0:T(256)S(1)} copy-done((f32[256]{0:T(256)S(1)}, f32[256]{0:T(256)}, u32[]{:S(2)}) %copy-start.4) | copy-done | bytes 1048
  5.8 0.0 copy-start.5
  5.8 0.7 %copy-done.5 = s32[8]{0:T(128)S(1)} copy-done((s32[8]{0:T(128)S(1)}, s32[8]{0:T(128)}, u32[]{:S(2)}) %copy-start.5) | copy-done | bytes 56
  6.4 34.3 %davidson_step.1 = (bf16[1024,256]{1,0:T(8,128)(2,1)S(1)}, bf16[1024,256]{1,0:T(8,128)(2,1)S(1)}, f32[64,512]{1,0:T(8,128)S(1)}, f32[64,512]{1,0:T(8,128)S(1)}, f32[1,256]{1,0:T(1,128)S(1)}) custom-call(s32[8,8]{1,0:T(8,128)S(1)} %copy-done.3, s32[8]{0:T(128)S(1)} %copy-done.5, bf16[1024,512]{1,0:T(8,128)(2,1)S(1)} %copy-done.1, ...), custom_call_target="tpu_custom_call" | custom-call | tf_op jit(solution)/shard_map/davidson_step/pallas_call | solution.py:308
  40.7 0.8 %copy.16 = bf16[1024,256]{1,0:T(8,128)(2,1)} copy(bf16[1024,256]{1,0:T(8,128)(2,1)S(1)} %get-tuple-element.20) | data formatting | bytes 1048576
  41.5 0.8 %copy.17 = bf16[1024,256]{1,0:T(8,128)(2,1)} copy(bf16[1024,256]{1,0:T(8,128)(2,1)S(1)} %get-tuple-element.21) | data formatting | bytes 1048576
  42.3 0.7 %copy.18 = f32[64,512]{1,0:T(8,128)} copy(f32[64,512]{1,0:T(8,128)S(1)} %get-tuple-element.22) | data formatting | bytes 262144
  43.0 0.7 %copy.19 = f32[64,512]{1,0:T(8,128)} copy(f32[64,512]{1,0:T(8,128)S(1)} %get-tuple-element.23) | data formatting | bytes 262144
  43.6 0.6 %copy.20 = f32[256]{0:T(256)} copy(f32[256]{0:T(256)S(1)} %bitcast.3) | data formatting | bytes 2048
Async XLA Ops:
  0.6 1.6 %copy-start = (bf16[8,8,128,128]{3,2,1,0:T(8,128)(2,1)S(1)}, bf16[8,8,128,128]{3,2,1,0:T(8,128)(2,1)}, u32[]{:S(2)}) copy-start(bf16[8,8,128,128]{3,2,1,0:T(8,128)(2,1)} %blocks_hbm.1) | copy-start | bytes 6291460
  2.2 1.2 %copy-start.1 = (bf16[1024,512]{1,0:T(8,128)(2,1)S(1)}, bf16[1024,512]{1,0:T(8,128)(2,1)}, u32[]{:S(2)}) copy-start(bf16[1024,512]{1,0:T(8,128)(2,1)} %basis_hbm.1) | copy-start | bytes 3145732
  3.5 0.9 %copy-start.2 = (bf16[512,256]{1,0:T(8,128)(2,1)S(1)}, bf16[512,256]{1,0:T(8,128)(2,1)}, u32[]{:S(2)}) copy-start(bf16[512,256]{1,0:T(8,128)(2,1)} %rot.1) | copy-start | bytes 786436
  4.4 0.7 %copy-start.3 = (s32[8,8]{1,0:T(8,128)S(1)}, s32[8,8]{1,0:T(8,128)}, u32[]{:S(2)}) copy-start(s32[8,8]{1,0:T(8,128)} %nbr.1) | copy-start | bytes 772
  5.1 0.7 %copy-start.4 = (f32[256]{0:T(256)S(1)}, f32[256]{0:T(256)}, u32[]{:S(2)}) copy-start(f32[256]{0:T(256)} %param.11) | copy-start | bytes 3076
  5.8 0.7 %copy-start.5 = (s32[8]{0:T(128)S(1)}, s32[8]{0:T(128)}, u32[]{:S(2)}) copy-start(s32[8]{0:T(128)} %cnt.1) | copy-start | bytes 100

commit v2 on v1

--- a/solution.py
+++ b/solution.py
@@ -77,6 +77,8 @@
 
 
 BF16, F32 = jnp.bfloat16, jnp.float32
+PARTS = 2
+SQ = 2 * PARTS
 
 
 def dot(a, b):
@@ -88,8 +90,9 @@
 
 
 def kernel(
-    sizes, nbr, cnt, basis_hbm, blocks_hbm, rot, vals,
-    ritz_hbm, rimg_hbm, gram_out, proj_out, res_out,
+    sizes, nbr, cnt, basis_hbm, blocks_hbm, rot_hbm, vals_hbm,
+    ritz_hbm, sums_out, res_out,
+    rot, vals,
     own, blk, mat_in, mat_halo, halo, acc, image, bt, rfull, ritz_v, rimg_v,
     half, core_send, core_recv, part, plane_send, plane_recv,
     z_send, z_recv, gat, sq_own, sq_core, sq_plane, sq_z,
@@ -124,6 +127,10 @@
     get_basis.start()
     get_blocks = pltpu.make_async_copy(blocks_hbm, blk, local_sem.at[1])
     get_blocks.start()
+    get_rot = pltpu.make_async_copy(rot_hbm, rot, local_sem.at[4])
+    get_rot.start()
+    get_vals = pltpu.make_async_copy(vals_hbm, vals, local_sem.at[5])
+    get_vals.start()
 
     barrier = pltpu.get_barrier_semaphore()
     peers = [ahead, behind, mate] + plane + line
@@ -155,18 +162,25 @@
         for side in range(2):
             bt[side, pl.ds(i * chunk, chunk), :] = turned[side * chunk:(side + 1) * chunk]
 
+    wide = k // PARTS
+
+    def columns(which):
+        return pl.ds((which % PARTS) * wide, wide)
+
     def core_phase(which, right):
-        core_send[which] = dot(bt[1 - c], right[...]).astype(BF16)
+        core_send[which] = dot(bt[1 - c], right[:, columns(which)]).astype(BF16)
         copy = remote(core_send.at[which], core_recv.at[which], core_ss.at[which],
                       core_rs.at[which], mate)
-        half[which] = dot(bt[c], right[...])
         return copy
+
+    def own_half(which, right):
+        half[which] = dot(bt[c], right[:, columns(which)])
 
     def plane_phase(which, core_copy):
         core_copy.wait_recv()
         total = half[which] + core_recv[which].astype(F32)
         half[which] = total
-        plane_send[which] = total.astype(BF16).reshape(Q, chunk, k)
+        plane_send[which] = total.astype(BF16).reshape(Q, chunk, wide)
         return [
             remote(plane_send.at[which, plane_q[d]], plane_recv.at[which, d],
                    plane_ss.at[which, d], plane_rs.at[which, d], plane[d])
@@ -179,7 +193,7 @@
             copy.wait_recv()
             total = total + plane_recv[which, d].astype(F32)
         part[which] = total
-        z_send[which] = total.astype(BF16).reshape(Z, piece, k)
+        z_send[which] = total.astype(BF16).reshape(Z, piece, wide)
         return [
             remote(z_send.at[which, line_z[d]], z_recv.at[which, d],
                    zs_ss.at[which, d], zs_rs.at[which, d], line[d])
@@ -198,16 +212,24 @@
             for d in range(Z - 1)
         ]
 
-    def finish(which, copies, out):
+    def finish(which, copies):
         for copy in copies:
             copy.wait_recv()
-        out[...] = gat[which].astype(F32).reshape(chunk, k) / rows_total
-
-    gram_core = core_phase(0, own)
-
+        sums_out[which // PARTS, :, columns(which)] = (
+            gat[which].astype(F32).reshape(chunk, wide) / rows_total
+        )
+
+    gram = range(PARTS)
+    proj = range(PARTS, 2 * PARTS)
+
+    gram_core = [core_phase(u, own) for u in gram]
+    for u in gram:
+        own_half(u, own)
+
+    get_rot.wait()
     rfull[...] = dot(own[...], rot[...])
     ritz_v[...] = rfull[...].astype(BF16)
-    put_ritz = pltpu.make_async_copy(ritz_v, ritz_hbm, local_sem.at[2])
+    put_ritz = pltpu.make_async_copy(ritz_v, ritz_hbm.at[0], local_sem.at[2])
     put_ritz.start()
 
     get_blocks.wait()
@@ -230,7 +252,7 @@
             else:
                 mat_in[there, (s - 1) * bs:s * bs] = total
 
-    gram_plane = plane_phase(0, gram_core)
+    gram_plane = [plane_phase(u, gram_core[u]) for u in gram]
 
     step = min(rows, 2 * bs)
 
@@ -239,7 +261,7 @@
         there = pl.ds(pl.multiple_of(i * step, step), step)
         acc[there, :] = dot(mat_in[there, :], own[...])
 
-    gram_line = line_phase(0, gram_plane)
+    gram_line = [line_phase(u, gram_plane[u]) for u in gram]
 
     for copy in halo_copies:
         copy.wait_recv()
@@ -249,8 +271,11 @@
         there = pl.ds(pl.multiple_of(i * step, step), step)
         image[there, :] = (acc[there, :] + dot(mat_halo[there, :], halo[...])).astype(BF16)
 
-    proj_core = core_phase(1, image)
-    gram_gather = gather_phase(0, gram_line)
+    proj_core = [core_phase(u, image) for u in proj]
+    for u in proj:
+        own_half(u, image)
+    proj_plane = [plane_phase(u, copy) for u, copy in zip(proj, proj_core)]
+    get_vals.wait()
 
     sq_own[...] = jnp.zeros_like(sq_own)
 
@@ -262,32 +287,34 @@
         resid = full - vals[...] * rfull[there, :]
         sq_own[...] += fold(resid * resid)
 
-    put_rimg = pltpu.make_async_copy(rimg_v, rimg_hbm, local_sem.at[3])
+    put_rimg = pltpu.make_async_copy(rimg_v, ritz_hbm.at[1], local_sem.at[3])
     put_rimg.start()
-    sq_copy = remote(sq_own, sq_core, core_ss.at[2], core_rs.at[2], mate)
-
-    proj_plane = plane_phase(1, proj_core)
+    sq_copy = remote(sq_own, sq_core, core_ss.at[SQ], core_rs.at[SQ], mate)
+
+    gram_gather = [gather_phase(u, gram_line[u]) for u in gram]
+    proj_line = [line_phase(u, copies) for u, copies in zip(proj, proj_plane)]
     sq_copy.wait_recv()
     sq_plane[q] = sq_own[...] + sq_core[...]
     sq_copies = [
-        remote(sq_plane.at[q], sq_plane.at[q], plane_ss.at[2, d], plane_rs.at[2, d], plane[d])
+        remote(sq_plane.at[q], sq_plane.at[q], plane_ss.at[SQ, d], plane_rs.at[SQ, d], plane[d])
         for d in range(Q - 1)
     ]
-    finish(0, gram_gather, gram_out)
-    proj_line = line_phase(1, proj_plane)
+    for u in gram:
+        finish(u, gram_gather[u])
+    proj_gather = [gather_phase(u, copies) for u, copies in zip(proj, proj_line)]
     for copy in sq_copies:
         copy.wait_recv()
     sq_z[z] = jnp.sum(sq_plane[...], axis=0)
     sq_copies = [
-        remote(sq_z.at[z], sq_z.at[z], za_ss.at[2, d], za_rs.at[2, d], line[d])
+        remote(sq_z.at[z], sq_z.at[z], za_ss.at[SQ, d], za_rs.at[SQ, d], line[d])
         for d in range(Z - 1)
     ]
-    proj_gather = gather_phase(1, proj_line)
+    for u, copies in zip(proj, proj_gather):
+        finish(u, copies)
     for copy in sq_copies:
         copy.wait_recv()
     squares = jnp.sum(jnp.sum(sq_z[...], axis=0), axis=0, keepdims=True)
     res_out[...] = jnp.sqrt(squares / rows_total)
-    finish(1, proj_gather, proj_out)
     for copy in sends:
         copy.wait_send()
     put_ritz.wait()
@@ -299,24 +326,24 @@
     nb, nnb, bs, _ = blocks.shape
     rows, k = basis.shape
     m = rotation.shape[1]
-    Q, chunk, piece = R // 2, k // R, k // R // Z
+    Q, chunk, piece, wide = R // 2, k // R, k // R // Z, k // PARTS
     vmem = pltpu.VMEM
     dma = pltpu.SemaphoreType.DMA
     any_spec = pl.BlockSpec(memory_space=pl.ANY)
     smem_spec = pl.BlockSpec(memory_space=pltpu.SMEM)
     vmem_spec = pl.BlockSpec(memory_space=pltpu.VMEM)
-    ritz, rimg, gram, proj, res = pl.pallas_call(
+    pair, sums, res = pl.pallas_call(
         functools.partial(kernel, (nb, nnb, bs, k, m, R, Z)),
         out_shape=(
-            jax.ShapeDtypeStruct((rows, m), BF16),
-            jax.ShapeDtypeStruct((rows, m), BF16),
-            jax.ShapeDtypeStruct((chunk, k), F32),
-            jax.ShapeDtypeStruct((chunk, k), F32),
+            jax.ShapeDtypeStruct((2, rows, m), BF16),
+            jax.ShapeDtypeStruct((2, chunk, k), F32),
             jax.ShapeDtypeStruct((1, m), F32),
         ),
-        in_specs=[smem_spec, smem_spec, any_spec, any_spec, vmem_spec, vmem_spec],
-        out_specs=(any_spec, any_spec, vmem_spec, vmem_spec, vmem_spec),
+        in_specs=[smem_spec, smem_spec, any_spec, any_spec, any_spec, any_spec],
+        out_specs=(any_spec, vmem_spec, vmem_spec),
         scratch_shapes=[
+            vmem((k, m), BF16),
+            vmem((1, m), F32),
             vmem((rows, k), BF16),
             vmem((nb, nnb, bs, bs), BF16),
             vmem((rows, nb * bs), BF16),
@@ -328,37 +355,37 @@
             vmem((rows, m), F32),
             vmem((rows, m), BF16),
             vmem((rows, m), BF16),
-            vmem((2, k // 2, k), F32),
-            vmem((2, k // 2, k), BF16),
-            vmem((2, k // 2, k), BF16),
-            vmem((2, chunk, k), F32),
-            vmem((2, Q, chunk, k), BF16),
-            vmem((2, Q - 1, chunk, k), BF16),
-            vmem((2, Z, piece, k), BF16),
-            vmem((2, Z - 1, piece, k), BF16),
-            vmem((2, Z, piece, k), BF16),
+            vmem((SQ, k // 2, wide), F32),
+            vmem((SQ, k // 2, wide), BF16),
+            vmem((SQ, k // 2, wide), BF16),
+            vmem((SQ, chunk, wide), F32),
+            vmem((SQ, Q, chunk, wide), BF16),
+            vmem((SQ, Q - 1, chunk, wide), BF16),
+            vmem((SQ, Z, piece, wide), BF16),
+            vmem((SQ, Z - 1, piece, wide), BF16),
+            vmem((SQ, Z, piece, wide), BF16),
             vmem((8, m), F32),
             vmem((8, m), F32),
             vmem((Q, 8, m), F32),
             vmem((Z, 8, m), F32),
-            dma((4,)),
+            dma((6,)),
             dma((2,)),
             dma((2,)),
-            dma((3,)),
-            dma((3,)),
-            dma((3, Q - 1)),
-            dma((3, Q - 1)),
-            dma((2, Z - 1)),
-            dma((2, Z - 1)),
-            dma((3, Z - 1)),
-            dma((3, Z - 1)),
+            dma((SQ + 1,)),
+            dma((SQ + 1,)),
+            dma((SQ + 1, Q - 1)),
+            dma((SQ + 1, Q - 1)),
+            dma((SQ, Z - 1)),
+            dma((SQ, Z - 1)),
+            dma((SQ + 1, Z - 1)),
+            dma((SQ + 1, Z - 1)),
         ],
         compiler_params=pltpu.CompilerParams(
-            collective_id=0, has_side_effects=True, vmem_limit_bytes=40 * 1024 * 1024
+            collective_id=0, has_side_effects=True, vmem_limit_bytes=62 * 1024 * 1024
         ),
         name="davidson_step",
     )(neighbours, counts, basis, blocks, rotation, ritz_values.reshape(1, m))
-    return ritz, rimg, gram, proj, res.reshape(m)
+    return pair[0], pair[1], sums[0], sums[1], res.reshape(m)
 
 
 def body(basis, blocks, neighbours, counts, rotation, ritz_values):

time: 44.4 us -> 37.7 us (0.85)
  local copies, waits for them, and re-layouts: 9.24 us -> 3.56 us
  Pallas kernels: 34.3 us -> 33.3 us
    unnamed x17 -> x5, local copies, waits for them, and re-layouts: 9.24 us -> 0.57 us
    squeeze x0 -> x2, local copies, waits for them, and re-layouts: none -> 2.99 us  [fused_body(): return (pair[0], pair[1], sums[0], sums[1], res.reshape(m))]
    pallas_call x1, Pallas kernels: 34.3 us -> 33.3 us  [fused_body(): pl.pallas_call(functools.partial(kernel, (nb, nnb, bs, k, m, R, Z)), out_...]
where the time goes in v2:
time: 37.7 us; the launch traced here: 37.5 us
  Pallas kernels  33.3 us (88%)
  local copies, waits for them, and re-layouts  3.56 us (9%)
  between operations  0.66 us (2%)
    pallas_call x1, Pallas kernels, fused_body(): pl.pallas_call(functools.partial(kernel, (nb, nnb, bs, k, m, R, Z)), out_...  33.3 us
    squeeze x2, local copies, waits for them, and re-layouts, fused_body(): return (pair[0], pair[1], sums[0], sums[1], res.reshape(m))  2.99 us

profile of v2, /device:TPU:0, one launch (start us, length us, event | category | flops | bytes accessed | tf_op | source)
XLA Modules:
  0.0 37.5 jit_solution(12369868266342738147)
XLA Ops:
  0.6 33.3 %davidson_step.1 = (bf16[2,1024,256]{2,1,0:T(8,128)(2,1)}, f32[2,64,512]{2,1,0:T(8,128)}, f32[1,256]{1,0:T(1,128)}) custom-call(s32[8,8]{1,0:T(8,128)} %nbr.1, s32[8]{0:T(128)} %cnt.1, bf16[1024,512]{1,0:T(8,128)(2,1)} %basis_hbm.1, bf16[8,8,128,128]{3,2,1,0:T(8,128)(2,1)} %blocks_hbm.1, bf16[512,256]{1,0:T(8,128)(2,1)} %rot_hbm.1, f32[1,256]{1,0:T(1,128)} %bitcast.10), custom_call_target="tpu_custom_call" | custom-call | tf_op jit(solution)/shard_map/davidson_step/pallas_call | solution.py:335
  34.0 0.0 copy-start
  34.0 0.0 copy-start.1
  34.0 2.3 %slice_bitcast_fusion = (bf16[1024,256]{1,0:T(8,128)(2,1)}, bf16[1024,256]{1,0:T(8,128)(2,1)}) fusion(bf16[2,1024,256]{2,1,0:T(8,128)(2,1)} %get-tuple-element.8), kind=kLoop, calls=%fused_computation | loop fusion | bytes 2097152 | tf_op jit(solution)/shard_map/squeeze | solution.py:388
  36.2 0.0 copy-done
  36.2 0.7 %slice_bitcast_fusion.2 = (f32[64,512]{1,0:T(8,128)}, f32[64,512]{1,0:T(8,128)}) fusion(f32[2,64,512]{2,1,0:T(8,128)S(1)} %copy-done), kind=kLoop, calls=%fused_computation.2 | loop fusion | bytes 524288 | tf_op jit(solution)/shard_map/squeeze | solution.py:388
  37.0 0.0 copy-done.1
  37.0 0.6 %copy.12 = f32[256]{0:T(256)} copy(f32[256]{0:T(256)S(1)} %bitcast.11) | data formatting | bytes 2048
Async XLA Ops:
  34.0 2.3 %copy-start = (f32[2,64,512]{2,1,0:T(8,128)S(1)}, f32[2,64,512]{2,1,0:T(8,128)}, u32[]{:S(2)}) copy-start(f32[2,64,512]{2,1,0:T(8,128)} %get-tuple-element.9) | copy-start | bytes 786436
  34.0 3.0 %copy-start.1 = (f32[1,256]{1,0:T(1,128)S(1)}, f32[1,256]{1,0:T(1,128)}, u32[]{:S(2)}) copy-start(f32[1,256]{1,0:T(1,128)} %get-tuple-element.10) | copy-start | bytes 3076

commit v3 on v2

--- a/solution.py
+++ b/solution.py
@@ -91,10 +91,10 @@
 
 def kernel(
     sizes, nbr, cnt, basis_hbm, blocks_hbm, rot_hbm, vals_hbm,
-    ritz_hbm, sums_out, res_out,
+    ritz_hbm, rimg_hbm, sums_out, res_out,
     rot, vals,
     own, blk, mat_in, mat_halo, halo, acc, image, bt, rfull, ritz_v, rimg_v,
-    half, core_send, core_recv, part, plane_send, plane_recv,
+    reach, ready, half, core_send, core_recv, part, plane_send, plane_recv,
     z_send, z_recv, gat, sq_own, sq_core, sq_plane, sq_z,
     local_sem, halo_ss, halo_rs, core_ss, core_rs, plane_ss, plane_rs,
     zs_ss, zs_rs, za_ss, za_rs,
@@ -167,14 +167,10 @@
     def columns(which):
         return pl.ds((which % PARTS) * wide, wide)
 
-    def core_phase(which, right):
-        core_send[which] = dot(bt[1 - c], right[:, columns(which)]).astype(BF16)
-        copy = remote(core_send.at[which], core_recv.at[which], core_ss.at[which],
+    def core_phase(which, values):
+        core_send[which] = values.astype(BF16)
+        return remote(core_send.at[which], core_recv.at[which], core_ss.at[which],
                       core_rs.at[which], mate)
-        return copy
-
-    def own_half(which, right):
-        half[which] = dot(bt[c], right[:, columns(which)])
 
     def plane_phase(which, core_copy):
         core_copy.wait_recv()
@@ -222,14 +218,14 @@
     gram = range(PARTS)
     proj = range(PARTS, 2 * PARTS)
 
-    gram_core = [core_phase(u, own) for u in gram]
+    gram_core = [core_phase(u, dot(bt[1 - c], own[:, columns(u)])) for u in gram]
     for u in gram:
-        own_half(u, own)
+        half[u] = dot(bt[c], own[:, columns(u)])
 
     get_rot.wait()
     rfull[...] = dot(own[...], rot[...])
     ritz_v[...] = rfull[...].astype(BF16)
-    put_ritz = pltpu.make_async_copy(ritz_v, ritz_hbm.at[0], local_sem.at[2])
+    put_ritz = pltpu.make_async_copy(ritz_v, ritz_hbm, local_sem.at[2])
     put_ritz.start()
 
     get_blocks.wait()
@@ -259,35 +255,41 @@
     @pl.loop(0, rows // step)
     def _(i):
         there = pl.ds(pl.multiple_of(i * step, step), step)
-        acc[there, :] = dot(mat_in[there, :], own[...])
-
-    gram_line = [line_phase(u, gram_plane[u]) for u in gram]
+        inside = dot(mat_in[there, :], own[...])
+        acc[there, :] = inside
+        image[there, :] = inside.astype(BF16)
+
+    for side in range(2):
+        reach[side] = dot(bt[side], mat_halo[...]).astype(BF16)
+    for u in proj:
+        ready[u - PARTS] = dot(bt[1 - c], image[:, columns(u)])
+    for u in proj:
+        half[u] = dot(bt[c], image[:, columns(u)])
 
     for copy in halo_copies:
         copy.wait_recv()
+
+    proj_core = [
+        core_phase(u, ready[u - PARTS] + dot(reach[1 - c], halo[:, columns(u)])) for u in proj
+    ]
+    for u in proj:
+        half[u] += dot(reach[c], halo[:, columns(u)])
+    gram_line = [line_phase(u, gram_plane[u]) for u in gram]
+    proj_plane = [plane_phase(u, copy) for u, copy in zip(proj, proj_core)]
+    get_vals.wait()
+
+    sq_own[...] = jnp.zeros_like(sq_own)
 
     @pl.loop(0, rows // step)
     def _(i):
         there = pl.ds(pl.multiple_of(i * step, step), step)
-        image[there, :] = (acc[there, :] + dot(mat_halo[there, :], halo[...])).astype(BF16)
-
-    proj_core = [core_phase(u, image) for u in proj]
-    for u in proj:
-        own_half(u, image)
-    proj_plane = [plane_phase(u, copy) for u, copy in zip(proj, proj_core)]
-    get_vals.wait()
-
-    sq_own[...] = jnp.zeros_like(sq_own)
-
-    @pl.loop(0, rows // step)
-    def _(i):
-        there = pl.ds(pl.multiple_of(i * step, step), step)
-        full = dot(image[there, :], rot[...])
+        outside = dot(mat_halo[there, :], halo[...])
+        full = dot((acc[there, :] + outside).astype(BF16), rot[...])
         rimg_v[there, :] = full.astype(BF16)
         resid = full - vals[...] * rfull[there, :]
         sq_own[...] += fold(resid * resid)
 
-    put_rimg = pltpu.make_async_copy(rimg_v, ritz_hbm.at[1], local_sem.at[3])
+    put_rimg = pltpu.make_async_copy(rimg_v, rimg_hbm, local_sem.at[3])
     put_rimg.start()
     sq_copy = remote(sq_own, sq_core, core_ss.at[SQ], core_rs.at[SQ], mate)
 
@@ -332,15 +334,16 @@
     any_spec = pl.BlockSpec(memory_space=pl.ANY)
     smem_spec = pl.BlockSpec(memory_space=pltpu.SMEM)
     vmem_spec = pl.BlockSpec(memory_space=pltpu.VMEM)
-    pair, sums, res = pl.pallas_call(
+    ritz, rimg, sums, res = pl.pallas_call(
         functools.partial(kernel, (nb, nnb, bs, k, m, R, Z)),
         out_shape=(
-            jax.ShapeDtypeStruct((2, rows, m), BF16),
+            jax.ShapeDtypeStruct((rows, m), BF16),
+            jax.ShapeDtypeStruct((rows, m), BF16),
             jax.ShapeDtypeStruct((2, chunk, k), F32),
             jax.ShapeDtypeStruct((1, m), F32),
         ),
         in_specs=[smem_spec, smem_spec, any_spec, any_spec, any_spec, any_spec],
-        out_specs=(any_spec, vmem_spec, vmem_spec),
+        out_specs=(any_spec, any_spec, vmem_spec, vmem_spec),
         scratch_shapes=[
             vmem((k, m), BF16),
             vmem((1, m), F32),
@@ -355,6 +358,8 @@
             vmem((rows, m), F32),
             vmem((rows, m), BF16),
             vmem((rows, m), BF16),
+            vmem((2, k // 2, 2 * bs), BF16),
+            vmem((PARTS, k // 2, wide), F32),
             vmem((SQ, k // 2, wide), F32),
             vmem((SQ, k // 2, wide), BF16),
             vmem((SQ, k // 2, wide), BF16),
@@ -385,7 +390,7 @@
         ),
         name="davidson_step",
     )(neighbours, counts, basis, blocks, rotation, ritz_values.reshape(1, m))
-    return pair[0], pair[1], sums[0], sums[1], res.reshape(m)
+    return ritz, rimg, sums[0], sums[1], res.reshape(m)
 
 
 def body(basis, blocks, neighbours, counts, rotation, ritz_values):

time: 37.7 us -> 37.3 us (0.989)
  Pallas kernels: 33.3 us -> 30.4 us
  local copies, waits for them, and re-layouts: 3.56 us -> 5.99 us
    unnamed x5, local copies, waits for them, and re-layouts: 0.57 us -> 4.3 us
    pallas_call x1, Pallas kernels: 33.3 us -> 30.4 us  [fused_body(): pl.pallas_call(functools.partial(kernel, (nb, nnb, bs, k, m, R, Z)), out_...]
    squeeze x2 -> x1, local copies, waits for them, and re-layouts: 2.99 us -> 1.69 us  [fused_body(): return (ritz, rimg, sums[0], sums[1], res.reshape(m))]
where the time goes in v3:
time: 37.3 us; the launch traced here: 37 us
  Pallas kernels  30.4 us (82%)
  local copies, waits for them, and re-layouts  5.99 us (16%)
  between operations  0.65 us (2%)
    pallas_call x1, Pallas kernels, fused_body(): pl.pallas_call(functools.partial(kernel, (nb, nnb, bs, k, m, R, Z)), out_...  30.4 us
    unnamed x5, local copies, waits for them, and re-layouts  4.3 us
    squeeze x1, local copies, waits for them, and re-layouts, fused_body(): return (ritz, rimg, sums[0], sums[1], res.reshape(m))  1.69 us

profile of v3, /device:TPU:0, one launch (start us, length us, event | category | flops | bytes accessed | tf_op | source)
XLA Modules:
  0.0 37.0 jit_solution(6426079691401681299)
XLA Ops:
  0.6 30.4 %davidson_step.1 = (bf16[1024,256]{1,0:T(8,128)(2,1)}, bf16[1024,256]{1,0:T(8,128)(2,1)}, f32[2,64,512]{2,1,0:T(8,128)}, f32[1,256]{1,0:T(1,128)}) custom-call(s32[8,8]{1,0:T(8,128)} %nbr.1, s32[8]{0:T(128)} %cnt.1, bf16[1024,512]{1,0:T(8,128)(2,1)} %basis_hbm.1, bf16[8,8,128,128]{3,2,1,0:T(8,128)(2,1)} %blocks_hbm.1, bf16[512,256]{1,0:T(8,128)(2,1)} %rot_hbm.1, ...), custom_call_target="tpu_custom_call" | custom-call | tf_op jit(solution)/shard_map/davidson_step/pallas_call | solution.py:337
  31.0 0.0 copy-start
  31.1 1.7 %slice_bitcast_fusion = (f32[64,512]{1,0:T(8,128)}, f32[64,512]{1,0:T(8,128)}) fusion(f32[2,64,512]{2,1,0:T(8,128)} %get-tuple-element.11), kind=kLoop, calls=%fused_computation | loop fusion | bytes 524288 | tf_op jit(solution)/shard_map/squeeze | solution.py:393
  32.7 1.9 %copy.14 = bf16[1024,256]{1,0:T(8,128)(2,1)} copy(bf16[1024,256]{1,0:T(8,128)(2,1)} %get-tuple-element.20) | data formatting | bytes 1048576
  34.6 1.9 %copy.15 = bf16[1024,256]{1,0:T(8,128)(2,1)} copy(bf16[1024,256]{1,0:T(8,128)(2,1)} %get-tuple-element.21) | data formatting | bytes 1048576
  36.5 0.0 copy-done
  36.5 0.6 %copy.16 = f32[256]{0:T(256)} copy(f32[256]{0:T(256)S(1)} %bitcast.7) | data formatting | bytes 2048
Async XLA Ops:
  31.0 5.4 %copy-start = (f32[1,256]{1,0:T(1,128)S(1)}, f32[1,256]{1,0:T(1,128)}, u32[]{:S(2)}) copy-start(f32[1,256]{1,0:T(1,128)} %get-tuple-element.12) | copy-start | bytes 3076

commit v4 on v3

--- a/solution.py
+++ b/solution.py
@@ -90,10 +90,10 @@
 
 
 def kernel(
-    sizes, nbr, cnt, basis_hbm, blocks_hbm, rot_hbm, vals_hbm,
-    ritz_hbm, rimg_hbm, sums_out, res_out,
-    rot, vals,
-    own, blk, mat_in, mat_halo, halo, acc, image, bt, rfull, ritz_v, rimg_v,
+    sizes, nbr_hbm, cnt_hbm, basis_hbm, blocks_hbm, rot_hbm, vals_hbm,
+    ritz_v, rimg_v, sums_out, res_out,
+    nbr, cnt, rot, vals,
+    own, blk, mat_in, mat_halo, halo, acc, image, bt, rfull,
     reach, ready, half, core_send, core_recv, part, plane_send, plane_recv,
     z_send, z_recv, gat, sq_own, sq_core, sq_plane, sq_z,
     local_sem, halo_ss, halo_rs, core_ss, core_rs, plane_ss, plane_rs,
@@ -127,6 +127,10 @@
     get_basis.start()
     get_blocks = pltpu.make_async_copy(blocks_hbm, blk, local_sem.at[1])
     get_blocks.start()
+    get_nbr = pltpu.make_async_copy(nbr_hbm, nbr, local_sem.at[2])
+    get_nbr.start()
+    get_cnt = pltpu.make_async_copy(cnt_hbm, cnt, local_sem.at[3])
+    get_cnt.start()
     get_rot = pltpu.make_async_copy(rot_hbm, rot, local_sem.at[4])
     get_rot.start()
     get_vals = pltpu.make_async_copy(vals_hbm, vals, local_sem.at[5])
@@ -225,14 +229,14 @@
     get_rot.wait()
     rfull[...] = dot(own[...], rot[...])
     ritz_v[...] = rfull[...].astype(BF16)
-    put_ritz = pltpu.make_async_copy(ritz_v, ritz_hbm, local_sem.at[2])
-    put_ritz.start()
 
     get_blocks.wait()
+    get_nbr.wait()
+    get_cnt.wait()
 
     @pl.loop(0, nb)
     def _(b):
-        n = cnt[b]
+        n = cnt[0, b]
         spot = [jnp.where(j < n, nbr[b, j] - first, -1) for j in range(nnb)]
         tiles = [blk[b, j] for j in range(nnb)]
         there = pl.ds(pl.multiple_of(b * bs, bs), bs)
@@ -289,8 +293,6 @@
         resid = full - vals[...] * rfull[there, :]
         sq_own[...] += fold(resid * resid)
 
-    put_rimg = pltpu.make_async_copy(rimg_v, rimg_hbm, local_sem.at[3])
-    put_rimg.start()
     sq_copy = remote(sq_own, sq_core, core_ss.at[SQ], core_rs.at[SQ], mate)
 
     gram_gather = [gather_phase(u, gram_line[u]) for u in gram]
@@ -319,8 +321,6 @@
     res_out[...] = jnp.sqrt(squares / rows_total)
     for copy in sends:
         copy.wait_send()
-    put_ritz.wait()
-    put_rimg.wait()
 
 
 def fused_body(basis, blocks, neighbours, counts, rotation, ritz_values):
@@ -331,8 +331,7 @@
     Q, chunk, piece, wide = R // 2, k // R, k // R // Z, k // PARTS
     vmem = pltpu.VMEM
     dma = pltpu.SemaphoreType.DMA
-    any_spec = pl.BlockSpec(memory_space=pl.ANY)
-    smem_spec = pl.BlockSpec(memory_space=pltpu.SMEM)
+    hbm_spec = pl.BlockSpec(memory_space=pltpu.HBM)
     vmem_spec = pl.BlockSpec(memory_space=pltpu.VMEM)
     ritz, rimg, sums, res = pl.pallas_call(
         functools.partial(kernel, (nb, nnb, bs, k, m, R, Z)),
@@ -342,9 +341,11 @@
             jax.ShapeDtypeStruct((2, chunk, k), F32),
             jax.ShapeDtypeStruct((1, m), F32),
         ),
-        in_specs=[smem_spec, smem_spec, any_spec, any_spec, any_spec, any_spec],
-        out_specs=(any_spec, any_spec, vmem_spec, vmem_spec),
+        in_specs=[hbm_spec] * 6,
+        out_specs=(vmem_spec,) * 4,
         scratch_shapes=[
+            pltpu.SMEM((nb, nnb), jnp.int32),
+            pltpu.SMEM((1, nb), jnp.int32),
             vmem((k, m), BF16),
             vmem((1, m), F32),
             vmem((rows, k), BF16),
@@ -356,8 +357,6 @@
             vmem((rows, k), BF16),
             vmem((2, k // 2, rows), BF16),
             vmem((rows, m), F32),
-            vmem((rows, m), BF16),
-            vmem((rows, m), BF16),
             vmem((2, k // 2, 2 * bs), BF16),
             vmem((PARTS, k // 2, wide), F32),
             vmem((SQ, k // 2, wide), F32),
@@ -386,10 +385,14 @@
             dma((SQ + 1, Z - 1)),
         ],
         compiler_params=pltpu.CompilerParams(
-            collective_id=0, has_side_effects=True, vmem_limit_bytes=62 * 1024 * 1024
+            collective_id=0, has_side_effects=True, vmem_limit_bytes=36 * 1024 * 1024
         ),
         name="davidson_step",
-    )(neighbours, counts, basis, blocks, rotation, ritz_values.reshape(1, m))
+    )(*[
+        pltpu.with_memory_space_constraint(x, pltpu.HBM)
+        for x in (neighbours, counts.reshape(1, nb), basis, blocks, rotation,
+                  ritz_values.reshape(1, m))
+    ])
     return ritz, rimg, sums[0], sums[1], res.reshape(m)
 
 

time: 37.3 us -> 32.6 us (0.87)
  local copies, waits for them, and re-layouts: 5.99 us -> 2.86 us
  Pallas kernels: 30.4 us -> 29 us
    unnamed x5 -> x3, local copies, waits for them, and re-layouts: 4.3 us -> 2.15 us
    pallas_call x1, Pallas kernels: 30.4 us -> 29 us  [fused_body(): pl.pallas_call(functools.partial(kernel, (nb, nnb, bs, k, m, R, Z)), out_...]
    squeeze x1, local copies, waits for them, and re-layouts: 1.69 us -> 0.72 us  [fused_body(): return (ritz, rimg, sums[0], sums[1], res.reshape(m))]
where the time goes in v4:
time: 32.6 us; the launch traced here: 32.5 us
  Pallas kernels  29 us (89%)
  local copies, waits for them, and re-layouts  2.86 us (9%)
  between operations  0.64 us (2%)
    pallas_call x1, Pallas kernels, fused_body(): pl.pallas_call(functools.partial(kernel, (nb, nnb, bs, k, m, R, Z)), out_...  29 us
    unnamed x3, local copies, waits for them, and re-layouts  2.15 us
    squeeze x1, local copies, waits for them, and re-layouts, fused_body(): return (ritz, rimg, sums[0], sums[1], res.reshape(m))  0.72 us

profile of v4, /device:TPU:0, one launch (start us, length us, event | category | flops | bytes accessed | tf_op | source)
XLA Modules:
  0.0 32.5 jit_solution(2520500699431067043)
XLA Ops:
  0.6 29.0 %davidson_step.1 = (bf16[1024,256]{1,0:T(8,128)(2,1)S(1)}, bf16[1024,256]{1,0:T(8,128)(2,1)S(1)}, f32[2,64,512]{2,1,0:T(8,128)S(1)}, f32[1,256]{1,0:T(1,128)S(1)}) custom-call(s32[8,8]{1,0:T(8,128)} %nbr_hbm.1, s32[1,8]{1,0:T(1,128)} %bitcast.9, bf16[1024,512]{1,0:T(8,128)(2,1)} %basis_hbm.1, bf16[8,8,128,128]{3,2,1,0:T(8,128)(2,1)} %blocks_hbm.1, ...), custom_call_target="tpu_custom_call" | custom-call | tf_op jit(solution)/shard_map/davidson_step/pallas_call | solution.py:336
  29.6 0.7 %slice_bitcast_fusion = (f32[64,512]{1,0:T(8,128)}, f32[64,512]{1,0:T(8,128)}) fusion(f32[2,64,512]{2,1,0:T(8,128)S(1)} %get-tuple-element.11), kind=kLoop, calls=%fused_computation | loop fusion | bytes 524288 | tf_op jit(solution)/shard_map/squeeze | solution.py:396
  30.3 0.8 %copy.14 = bf16[1024,256]{1,0:T(8,128)(2,1)} copy(bf16[1024,256]{1,0:T(8,128)(2,1)S(1)} %get-tuple-element.20) | data formatting | bytes 1048576
  31.1 0.8 %copy.15 = bf16[1024,256]{1,0:T(8,128)(2,1)} copy(bf16[1024,256]{1,0:T(8,128)(2,1)S(1)} %get-tuple-element.21) | data formatting | bytes 1048576
  31.9 0.6 %copy.16 = f32[256]{0:T(256)} copy(f32[256]{0:T(256)S(1)} %bitcast.7) | data formatting | bytes 2048

commit v5 on v4

--- a/solution.py
+++ b/solution.py
@@ -95,7 +95,7 @@
     nbr, cnt, rot, vals,
     own, blk, mat_in, mat_halo, halo, acc, image, bt, rfull,
     reach, ready, half, core_send, core_recv, part, plane_send, plane_recv,
-    z_send, z_recv, gat, sq_own, sq_core, sq_plane, sq_z,
+    z_send, z_recv, gat, spread, sq_own, sq_core, sq_plane, sq_z,
     local_sem, halo_ss, halo_rs, core_ss, core_rs, plane_ss, plane_rs,
     zs_ss, zs_rs, za_ss, za_rs,
 ):
@@ -200,6 +200,19 @@
             for d in range(Z - 1)
         ]
 
+    def spread_phase(which, copies):
+        total = half[which, pl.ds(pl.multiple_of(q * chunk, chunk), chunk), :]
+        for d, copy in enumerate(copies):
+            copy.wait_recv()
+            total = total + plane_recv[which, d].astype(F32)
+        u = which - PARTS
+        spread[u, z] = total.astype(BF16)
+        return [
+            remote(spread.at[u, z], spread.at[u, z],
+                   zs_ss.at[which, d], zs_rs.at[which, d], line[d])
+            for d in range(Z - 1)
+        ]
+
     def gather_phase(which, copies):
         total = part[which, pl.ds(pl.multiple_of(z * piece, piece), piece), :]
         for d, copy in enumerate(copies):
@@ -229,6 +242,8 @@
     get_rot.wait()
     rfull[...] = dot(own[...], rot[...])
     ritz_v[...] = rfull[...].astype(BF16)
+
+    gram_plane = [plane_phase(u, gram_core[u]) for u in gram]
 
     get_blocks.wait()
     get_nbr.wait()
@@ -252,7 +267,6 @@
             else:
                 mat_in[there, (s - 1) * bs:s * bs] = total
 
-    gram_plane = [plane_phase(u, gram_core[u]) for u in gram]
 
     step = min(rows, 2 * bs)
 
@@ -296,7 +310,7 @@
     sq_copy = remote(sq_own, sq_core, core_ss.at[SQ], core_rs.at[SQ], mate)
 
     gram_gather = [gather_phase(u, gram_line[u]) for u in gram]
-    proj_line = [line_phase(u, copies) for u, copies in zip(proj, proj_plane)]
+    proj_spread = [spread_phase(u, copies) for u, copies in zip(proj, proj_plane)]
     sq_copy.wait_recv()
     sq_plane[q] = sq_own[...] + sq_core[...]
     sq_copies = [
@@ -305,7 +319,6 @@
     ]
     for u in gram:
         finish(u, gram_gather[u])
-    proj_gather = [gather_phase(u, copies) for u, copies in zip(proj, proj_line)]
     for copy in sq_copies:
         copy.wait_recv()
     sq_z[z] = jnp.sum(sq_plane[...], axis=0)
@@ -313,8 +326,11 @@
         remote(sq_z.at[z], sq_z.at[z], za_ss.at[SQ, d], za_rs.at[SQ, d], line[d])
         for d in range(Z - 1)
     ]
-    for u, copies in zip(proj, proj_gather):
-        finish(u, copies)
+    for u, copies in zip(proj, proj_spread):
+        for copy in copies:
+            copy.wait_recv()
+        total = jnp.sum(spread[u - PARTS].astype(F32), axis=0)
+        sums_out[1, :, columns(u)] = total / rows_total
     for copy in sq_copies:
         copy.wait_recv()
     squares = jnp.sum(jnp.sum(sq_z[...], axis=0), axis=0, keepdims=True)
@@ -362,12 +378,13 @@
             vmem((SQ, k // 2, wide), F32),
             vmem((SQ, k // 2, wide), BF16),
             vmem((SQ, k // 2, wide), BF16),
-            vmem((SQ, chunk, wide), F32),
+            vmem((PARTS, chunk, wide), F32),
             vmem((SQ, Q, chunk, wide), BF16),
             vmem((SQ, Q - 1, chunk, wide), BF16),
-            vmem((SQ, Z, piece, wide), BF16),
-            vmem((SQ, Z - 1, piece, wide), BF16),
-            vmem((SQ, Z, piece, wide), BF16),
+            vmem((PARTS, Z, piece, wide), BF16),
+            vmem((PARTS, Z - 1, piece, wide), BF16),
+            vmem((PARTS, Z, piece, wide), BF16),
+            vmem((PARTS, Z, chunk, wide), BF16),
             vmem((8, m), F32),
             vmem((8, m), F32),
             vmem((Q, 8, m), F32),

time: 32.6 us -> 32.7 us (level)
  no operation moved by 1% of the time
where the time goes in v5:
time: 32.7 us; the launch traced here: 32.5 us
  Pallas kernels  29 us (89%)
  local copies, waits for them, and re-layouts  2.86 us (9%)
  between operations  0.64 us (2%)
    pallas_call x1, Pallas kernels, fused_body(): pl.pallas_call(functools.partial(kernel, (nb, nnb, bs, k, m, R, Z)), out_...  29 us
    unnamed x3, local copies, waits for them, and re-layouts  2.15 us
    squeeze x1, local copies, waits for them, and re-layouts, fused_body(): return (ritz, rimg, sums[0], sums[1], res.reshape(m))  0.72 us

profile of v5, /device:TPU:0, one launch (start us, length us, event | category | flops | bytes accessed | tf_op | source)
XLA Modules:
  0.0 32.5 jit_solution(5188946415487400309)
XLA Ops:
  0.6 29.0 %davidson_step.1 = (bf16[1024,256]{1,0:T(8,128)(2,1)S(1)}, bf16[1024,256]{1,0:T(8,128)(2,1)S(1)}, f32[2,64,512]{2,1,0:T(8,128)S(1)}, f32[1,256]{1,0:T(1,128)S(1)}) custom-call(s32[8,8]{1,0:T(8,128)} %nbr_hbm.1, s32[1,8]{1,0:T(1,128)} %bitcast.9, bf16[1024,512]{1,0:T(8,128)(2,1)} %basis_hbm.1, bf16[8,8,128,128]{3,2,1,0:T(8,128)(2,1)} %blocks_hbm.1, ...), custom_call_target="tpu_custom_call" | custom-call | tf_op jit(solution)/shard_map/davidson_step/pallas_call | solution.py:352
  29.7 0.7 %slice_bitcast_fusion = (f32[64,512]{1,0:T(8,128)}, f32[64,512]{1,0:T(8,128)}) fusion(f32[2,64,512]{2,1,0:T(8,128)S(1)} %get-tuple-element.11), kind=kLoop, calls=%fused_computation | loop fusion | bytes 524288 | tf_op jit(solution)/shard_map/squeeze | solution.py:413
  30.4 0.8 %copy.14 = bf16[1024,256]{1,0:T(8,128)(2,1)} copy(bf16[1024,256]{1,0:T(8,128)(2,1)S(1)} %get-tuple-element.20) | data formatting | bytes 1048576
  31.2 0.8 %copy.15 = bf16[1024,256]{1,0:T(8,128)(2,1)} copy(bf16[1024,256]{1,0:T(8,128)(2,1)S(1)} %get-tuple-element.21) | data formatting | bytes 1048576
  32.0 0.6 %copy.16 = f32[256]{0:T(256)} copy(f32[256]{0:T(256)S(1)} %bitcast.7) | data formatting | bytes 2048

commit v6 on v4

--- a/solution.py
+++ b/solution.py
@@ -222,13 +222,21 @@
     gram = range(PARTS)
     proj = range(PARTS, 2 * PARTS)
 
-    gram_core = [core_phase(u, dot(bt[1 - c], own[:, columns(u)])) for u in gram]
+    def both_halves(which, right):
+        left = bt[...].reshape(k, rows)
+        ready[which] = dot(left, right[:, columns(which)]).reshape(2, k // 2, wide)
+
+    gram_core = []
     for u in gram:
-        half[u] = dot(bt[c], own[:, columns(u)])
+        both_halves(u, own)
+        gram_core.append(core_phase(u, ready[u, 1 - c]))
+        half[u] = ready[u, c]
 
     get_rot.wait()
     rfull[...] = dot(own[...], rot[...])
     ritz_v[...] = rfull[...].astype(BF16)
+
+    gram_plane = [plane_phase(u, gram_core[u]) for u in gram]
 
     get_blocks.wait()
     get_nbr.wait()
@@ -252,9 +260,8 @@
             else:
                 mat_in[there, (s - 1) * bs:s * bs] = total
 
-    gram_plane = [plane_phase(u, gram_core[u]) for u in gram]
-
-    step = min(rows, 2 * bs)
+
+    step = min(rows, 4 * bs)
 
     @pl.loop(0, rows // step)
     def _(i):
@@ -263,21 +270,18 @@
         acc[there, :] = inside
         image[there, :] = inside.astype(BF16)
 
-    for side in range(2):
-        reach[side] = dot(bt[side], mat_halo[...]).astype(BF16)
+    reach[...] = dot(bt[...].reshape(k, rows), mat_halo[...]).astype(BF16).reshape(reach.shape)
     for u in proj:
-        ready[u - PARTS] = dot(bt[1 - c], image[:, columns(u)])
-    for u in proj:
-        half[u] = dot(bt[c], image[:, columns(u)])
+        both_halves(u, image)
 
     for copy in halo_copies:
         copy.wait_recv()
 
     proj_core = [
-        core_phase(u, ready[u - PARTS] + dot(reach[1 - c], halo[:, columns(u)])) for u in proj
+        core_phase(u, ready[u, 1 - c] + dot(reach[1 - c], halo[:, columns(u)])) for u in proj
     ]
     for u in proj:
-        half[u] += dot(reach[c], halo[:, columns(u)])
+        half[u] = ready[u, c] + dot(reach[c], halo[:, columns(u)])
     gram_line = [line_phase(u, gram_plane[u]) for u in gram]
     proj_plane = [plane_phase(u, copy) for u, copy in zip(proj, proj_core)]
     get_vals.wait()
@@ -358,7 +362,7 @@
             vmem((2, k // 2, rows), BF16),
             vmem((rows, m), F32),
             vmem((2, k // 2, 2 * bs), BF16),
-            vmem((PARTS, k // 2, wide), F32),
+            vmem((SQ, 2, k // 2, wide), F32),
             vmem((SQ, k // 2, wide), F32),
             vmem((SQ, k // 2, wide), BF16),
             vmem((SQ, k // 2, wide), BF16),
@@ -400,6 +404,7 @@
     R, Z = lax.axis_size("rows"), lax.axis_size("cols")
     k = basis.shape[1]
     even = R % 4 == 0 and Z > 1 and k % (16 * R * Z) == 0 and (2 * k // R) % 128 == 0
+    even = even and blocks.shape[0] % 4 == 0 and k % (256 * PARTS) == 0
     chosen = fused_body if even else general_body
     return chosen(basis, blocks, neighbours, counts, rotation, ritz_values)
 

time: 32.6 us -> 32.8 us (level)
  no operation moved by 1% of the time
where the time goes in v6:
time: 32.8 us; the launch traced here: 32.7 us
  Pallas kernels  29.2 us (89%)
  local copies, waits for them, and re-layouts  2.86 us (9%)
  between operations  0.64 us (2%)
    pallas_call x1, Pallas kernels, fused_body(): pl.pallas_call(functools.partial(kernel, (nb, nnb, bs, k, m, R, Z)), out_...  29.2 us
    unnamed x3, local copies, waits for them, and re-layouts  2.15 us
    squeeze x1, local copies, waits for them, and re-layouts, fused_body(): return (ritz, rimg, sums[0], sums[1], res.reshape(m))  0.72 us

profile of v6, /device:TPU:0, one launch (start us, length us, event | category | flops | bytes accessed | tf_op | source)
XLA Modules:
  0.0 32.7 jit_solution(9333898723785542385)
XLA Ops:
  0.6 29.2 %davidson_step.1 = (bf16[1024,256]{1,0:T(8,128)(2,1)S(1)}, bf16[1024,256]{1,0:T(8,128)(2,1)S(1)}, f32[2,64,512]{2,1,0:T(8,128)S(1)}, f32[1,256]{1,0:T(1,128)S(1)}) custom-call(s32[8,8]{1,0:T(8,128)} %nbr_hbm.1, s32[1,8]{1,0:T(1,128)} %bitcast.9, bf16[1024,512]{1,0:T(8,128)(2,1)} %basis_hbm.1, bf16[8,8,128,128]{3,2,1,0:T(8,128)(2,1)} %blocks_hbm.1, ...), custom_call_target="tpu_custom_call" | custom-call | tf_op jit(solution)/shard_map/davidson_step/pallas_call | solution.py:340
  29.8 0.7 %slice_bitcast_fusion = (f32[64,512]{1,0:T(8,128)}, f32[64,512]{1,0:T(8,128)}) fusion(f32[2,64,512]{2,1,0:T(8,128)S(1)} %get-tuple-element.11), kind=kLoop, calls=%fused_computation | loop fusion | bytes 524288 | tf_op jit(solution)/shard_map/squeeze | solution.py:400
  30.5 0.8 %copy.14 = bf16[1024,256]{1,0:T(8,128)(2,1)} copy(bf16[1024,256]{1,0:T(8,128)(2,1)S(1)} %get-tuple-element.20) | data formatting | bytes 1048576
  31.3 0.8 %copy.15 = bf16[1024,256]{1,0:T(8,128)(2,1)} copy(bf16[1024,256]{1,0:T(8,128)(2,1)S(1)} %get-tuple-element.21) | data formatting | bytes 1048576
  32.1 0.6 %copy.16 = f32[256]{0:T(256)} copy(f32[256]{0:T(256)S(1)} %bitcast.7) | data formatting | bytes 2048

commit v7 on v4

--- a/solution.py
+++ b/solution.py
@@ -230,6 +230,8 @@
     rfull[...] = dot(own[...], rot[...])
     ritz_v[...] = rfull[...].astype(BF16)
 
+    gram_plane = [plane_phase(u, gram_core[u]) for u in gram]
+
     get_blocks.wait()
     get_nbr.wait()
     get_cnt.wait()
@@ -252,7 +254,6 @@
             else:
                 mat_in[there, (s - 1) * bs:s * bs] = total
 
-    gram_plane = [plane_phase(u, gram_core[u]) for u in gram]
 
     step = min(rows, 2 * bs)
 
@@ -276,16 +277,15 @@
     proj_core = [
         core_phase(u, ready[u - PARTS] + dot(reach[1 - c], halo[:, columns(u)])) for u in proj
     ]
+    gram_line = [line_phase(u, gram_plane[u]) for u in gram]
     for u in proj:
         half[u] += dot(reach[c], halo[:, columns(u)])
-    gram_line = [line_phase(u, gram_plane[u]) for u in gram]
     proj_plane = [plane_phase(u, copy) for u, copy in zip(proj, proj_core)]
     get_vals.wait()
 
     sq_own[...] = jnp.zeros_like(sq_own)
 
-    @pl.loop(0, rows // step)
-    def _(i):
+    def rotate(i):
         there = pl.ds(pl.multiple_of(i * step, step), step)
         outside = dot(mat_halo[there, :], halo[...])
         full = dot((acc[there, :] + outside).astype(BF16), rot[...])
@@ -293,9 +293,13 @@
         resid = full - vals[...] * rfull[there, :]
         sq_own[...] += fold(resid * resid)
 
+    middle = rows // step // 2
+    pl.loop(0, middle)(rotate)
+    gram_gather = [gather_phase(u, gram_line[u]) for u in gram]
+    pl.loop(middle, rows // step)(rotate)
+
     sq_copy = remote(sq_own, sq_core, core_ss.at[SQ], core_rs.at[SQ], mate)
 
-    gram_gather = [gather_phase(u, gram_line[u]) for u in gram]
     proj_line = [line_phase(u, copies) for u, copies in zip(proj, proj_plane)]
     sq_copy.wait_recv()
     sq_plane[q] = sq_own[...] + sq_core[...]

time: 32.6 us -> 32.5 us (level)
  no operation moved by 1% of the time
where the time goes in v7:
time: 32.5 us; the launch traced here: 32.3 us
  Pallas kernels  28.8 us (89%)
  local copies, waits for them, and re-layouts  2.86 us (9%)
  between operations  0.64 us (2%)
    pallas_call x1, Pallas kernels, fused_body(): pl.pallas_call(functools.partial(kernel, (nb, nnb, bs, k, m, R, Z)), out_...  28.8 us
    unnamed x3, local copies, waits for them, and re-layouts  2.15 us
    squeeze x1, local copies, waits for them, and re-layouts, fused_body(): return (ritz, rimg, sums[0], sums[1], res.reshape(m))  0.72 us

profile of v7, /device:TPU:0, one launch (start us, length us, event | category | flops | bytes accessed | tf_op | source)
XLA Modules:
  0.0 32.3 jit_solution(889448096926507548)
XLA Ops:
  0.6 28.8 %davidson_step.1 = (bf16[1024,256]{1,0:T(8,128)(2,1)S(1)}, bf16[1024,256]{1,0:T(8,128)(2,1)S(1)}, f32[2,64,512]{2,1,0:T(8,128)S(1)}, f32[1,256]{1,0:T(1,128)S(1)}) custom-call(s32[8,8]{1,0:T(8,128)} %nbr_hbm.1, s32[1,8]{1,0:T(1,128)} %bitcast.9, bf16[1024,512]{1,0:T(8,128)(2,1)} %basis_hbm.1, bf16[8,8,128,128]{3,2,1,0:T(8,128)(2,1)} %blocks_hbm.1, ...), custom_call_target="tpu_custom_call" | custom-call | tf_op jit(solution)/shard_map/davidson_step/pallas_call | solution.py:340
  29.5 0.7 %slice_bitcast_fusion = (f32[64,512]{1,0:T(8,128)}, f32[64,512]{1,0:T(8,128)}) fusion(f32[2,64,512]{2,1,0:T(8,128)S(1)} %get-tuple-element.11), kind=kLoop, calls=%fused_computation | loop fusion | bytes 524288 | tf_op jit(solution)/shard_map/squeeze | solution.py:400
  30.2 0.8 %copy.14 = bf16[1024,256]{1,0:T(8,128)(2,1)} copy(bf16[1024,256]{1,0:T(8,128)(2,1)S(1)} %get-tuple-element.20) | data formatting | bytes 1048576
  31.0 0.8 %copy.15 = bf16[1024,256]{1,0:T(8,128)(2,1)} copy(bf16[1024,256]{1,0:T(8,128)(2,1)S(1)} %get-tuple-element.21) | data formatting | bytes 1048576
  31.8 0.6 %copy.16 = f32[256]{0:T(256)} copy(f32[256]{0:T(256)S(1)} %bitcast.7) | data formatting | bytes 2048

commit v8 on v7

--- a/solution.py
+++ b/solution.py
@@ -77,7 +77,7 @@
 
 
 BF16, F32 = jnp.bfloat16, jnp.float32
-PARTS = 2
+PARTS = 1
 SQ = 2 * PARTS
 
 

time: 32.5 us -> 32.3 us (level)
  no operation moved by 1% of the time
where the time goes in v8:
time: 32.3 us; the launch traced here: 32.2 us
  Pallas kernels  28.7 us (89%)
  local copies, waits for them, and re-layouts  2.86 us (9%)
  between operations  0.64 us (2%)
    pallas_call x1, Pallas kernels, fused_body(): pl.pallas_call(functools.partial(kernel, (nb, nnb, bs, k, m, R, Z)), out_...  28.7 us
    unnamed x3, local copies, waits for them, and re-layouts  2.15 us
    squeeze x1, local copies, waits for them, and re-layouts, fused_body(): return (ritz, rimg, sums[0], sums[1], res.reshape(m))  0.72 us

profile of v8, /device:TPU:0, one launch (start us, length us, event | category | flops | bytes accessed | tf_op | source)
XLA Modules:
  0.0 32.2 jit_solution(14744243375401445311)
XLA Ops:
  0.6 28.7 %davidson_step.1 = (bf16[1024,256]{1,0:T(8,128)(2,1)S(1)}, bf16[1024,256]{1,0:T(8,128)(2,1)S(1)}, f32[2,64,512]{2,1,0:T(8,128)S(1)}, f32[1,256]{1,0:T(1,128)S(1)}) custom-call(s32[8,8]{1,0:T(8,128)} %nbr_hbm.1, s32[1,8]{1,0:T(1,128)} %bitcast.9, bf16[1024,512]{1,0:T(8,128)(2,1)} %basis_hbm.1, bf16[8,8,128,128]{3,2,1,0:T(8,128)(2,1)} %blocks_hbm.1, ...), custom_call_target="tpu_custom_call" | custom-call | tf_op jit(solution)/shard_map/davidson_step/pallas_call | solution.py:340
  29.3 0.7 %slice_bitcast_fusion = (f32[64,512]{1,0:T(8,128)}, f32[64,512]{1,0:T(8,128)}) fusion(f32[2,64,512]{2,1,0:T(8,128)S(1)} %get-tuple-element.11), kind=kLoop, calls=%fused_computation | loop fusion | bytes 524288 | tf_op jit(solution)/shard_map/squeeze | solution.py:400
  30.0 0.8 %copy.14 = bf16[1024,256]{1,0:T(8,128)(2,1)} copy(bf16[1024,256]{1,0:T(8,128)(2,1)S(1)} %get-tuple-element.20) | data formatting | bytes 1048576
  30.8 0.8 %copy.15 = bf16[1024,256]{1,0:T(8,128)(2,1)} copy(bf16[1024,256]{1,0:T(8,128)(2,1)S(1)} %get-tuple-element.21) | data formatting | bytes 1048576
  31.6 0.6 %copy.16 = f32[256]{0:T(256)} copy(f32[256]{0:T(256)S(1)} %bitcast.7) | data formatting | bytes 2048
